TPU v7x, 128 devices: a whole 4x4x4 slice. The times are simulated.
128 devices in a mesh: ctg: 16 (over y, x), line: 8 (over z, core).
Axes of the slice: x: 4, y: 4, z: 4, core: 2. Of those that a mesh axis runs over, the one named last changes fastest.
Arguments:
- base_flow: float32 [384, 15360], P(None, ('ctg', 'line')), may hold values from -6 to 6
- lodf: bfloat16 [15360, 15360], P('line', 'ctg'), may hold values from -0.3125 to 0.3125
- dual: bfloat16 [15360, 15360], P('line', 'ctg'), may hold values from 0 to 2.5, as said below
- rating: float32 [15360], P('line'), may hold values from 0.3 to 2
- sens: bfloat16 [15360, 2048], P('line', 'ctg'), may hold values from -0.046875 to 0.046875
- fetch_rows: int32 [16, 128, 15], P('ctg'), may hold values from -1 to 119, as said below
- ctg_slot: int32 [15360], P('ctg'), may hold values from 0 to 1919, as said below
Outputs:
- cut: float32 [2048, 384], P(('ctg', 'line'))
Inputs may be any that keep to these rules, and one draw needn't show every extreme that they name: `fetch_rows`: -1 marks an empty slot; other entries are distinct columns of flow holder o's block of 120 lines; some pairs (c, o) may have no live slot, and one flow holder has all 15 slots live for every contingency holder. `ctg_slot`: the 960 contingencies of holder c take distinct slots o * 15 + j, exactly the live entries of fetch_rows[c]. `dual`: zero outside the overloaded pairs, positive on them.
All inputs are finite; a program needn't handle non-finite values.
Results may differ from a plain program's by a relative error of at most 0.0059.
Values may be sent and summed in bfloat16 or wider, within the bound.
A program may use at most 64 MiB of HBM per device.

v0:
```python
import jax
import jax.numpy as jnp
from jax import lax
from jax.sharding import PartitionSpec as P


def soft_excess(flow_sum, rating):
    return jnp.sign(flow_sum) * jnp.maximum(jnp.abs(flow_sum) - rating[None, :], 0.0)


def per_device(base_flow, lodf, dual, rating, sens, fetch_rows, ctg_slot):
    columns_total = base_flow.shape[0]
    requests = fetch_rows[0]
    asked = lax.all_to_all(requests, ("ctg", "line"), split_axis=0, concat_axis=0, tiled=True)
    live_slot = asked >= 0
    columns = jnp.where(live_slot, asked, 0)
    values = jnp.take(base_flow, columns.reshape(-1), axis=1)
    values = values.reshape(columns_total, asked.shape[0], asked.shape[1])
    replies = lax.all_to_all(
        jnp.where(live_slot[None], values, 0.0).astype(jnp.bfloat16),
        ("ctg", "line"),
        split_axis=1,
        concat_axis=1,
        tiled=True,
    )
    slot_flows = replies.reshape(columns_total, -1)
    outage_flow = jnp.take(slot_flows, ctg_slot, axis=1)
    weighted = (dual.astype(jnp.float32) * lodf.astype(jnp.float32)).astype(jnp.bfloat16)
    partial_value = lax.dot_general(
        outage_flow, weighted, (((1,), (1,)), ((), ())), preferred_element_type=jnp.float32
    )
    totals = lax.psum(partial_value, "ctg")
    excess = soft_excess(totals, rating).astype(jnp.bfloat16)
    columns = sens
    return lax.psum_scatter(
        lax.dot_general(
            columns, excess, (((0,), (1,)), ((), ())), preferred_element_type=jnp.float32
        ),
        "line",
        scatter_dimension=0,
        tiled=True,
    )


def solution(mesh):
    in_specs = (
        P(None, ("ctg", "line")),
        P("line", "ctg"),
        P("line", "ctg"),
        P("line"),
        P("line", "ctg"),
        P("ctg", None, None),
        P("ctg"),
    )
    out_specs = P(("ctg", "line"), None)
    return jax.shard_map(
        per_device, mesh=mesh, in_specs=in_specs, out_specs=out_specs, check_vma=False
    )
```

profile of v0, /device:TPU:0, one launch (start us, length us, event | category | flops | bytes accessed | tf_op | source)
XLA Modules:
  0.0 210.2 jit_solution(16124836973732095510)
XLA Ops:
  6.5 0.9 copy.22
  7.4 20.5 %all_to_all.20 = s32[128,1,15]{2,1,0:T(1,128)S(1)} all-to-all(s32[128,1,15]{2,1,0:T(1,128)S(1)} %copy.22), channel_id=1, replica_groups=mesh['ctg'=16,'line'=8] {'ctg','line'}, dimensions={0} | all-to-all | bytes 15360 | tf_op jit(solution)/shard_map/all_to_all | solution.py:14
  27.9 0.1 copy.23
  28.0 0.5 broadcast.84
  28.5 0.8 reduce.5
  29.3 0.2 all_to_all.16
  29.6 0.1 copy.24
  29.7 0.7 copy.25
  30.4 5.0 %gather_fusion = bf16[1920,384]{1,0:T(8,128)(2,1)S(1)} fusion(f32[384,120]{0,1:T(8,128)S(1)} %copy-done.1, s32[2048]{0:T(1024)S(1)} %pad_clamp_fusion), kind=kCustom, calls=%fused_computation | custom fusion | bytes 2956800 | tf_op jit(solution)/shard_map/jit(_take)/gather | solution.py:17
  35.5 0.5 gather.11
  36.0 3.1 %select_convert_fusion = bf16[384,128,15]{0,2,1:T(8,128)(2,1)} fusion(bf16[384,128,15]{0,2,1:T(8,128)(2,1)S(1)} %gather.11, pred[128,15]{1,0:T(8,128)(4,1)} %copy.25, pred[128,15]{1,0:T(8,128)(4,1)S(1)} %copy.24), kind=kLoop, calls=%fused_computation.4 | loop fusion | flops 1474560 | bytes 2952960 | tf_op jit(solution)/shard_map/convert_element_type | solution.py:20
  39.1 4.6 %all-to-all-start.1 = ((bf16[384,128,15]{0,2,1:T(8,128)(2,1)}), bf16[384,128,15]{0,2,1:T(8,128)(2,1)S(1)}, u32[]{:S(2)}, u32[]{:S(2)}) async-start(bf16[384,128,15]{0,2,1:T(8,128)(2,1)} %select_convert_fusion), calls=%async_computation.1 | async-start | bytes 3145728 | tf_op jit(solution)/shard_map/all_to_all | solution.py:19
  43.7 0.0 all-reduce.2.cloned.1.call-start
  43.8 24.8 %all-to-all-done.1 = bf16[384,128,15]{0,2,1:T(8,128)(2,1)S(1)} async-done(((bf16[384,128,15]{0,2,1:T(8,128)(2,1)}), bf16[384,128,15]{0,2,1:T(8,128)(2,1)S(1)}, u32[]{:S(2)}, u32[]{:S(2)}) %all-to-all-start.1) | async-done | bytes 1474592 | tf_op jit(solution)/shard_map/all_to_all | solution.py:19
  68.6 0.5 reshape.60
  69.1 4.1 %gather_fusion.1 = bf16[960,384]{1,0:T(8,128)(2,1)S(1)} fusion(bf16[384,1920]{0,1:T(8,128)(2,1)S(1)} %reshape.60, s32[1024]{0:T(1024)S(1)} %pad_clamp_fusion.1), kind=kCustom, calls=%fused_computation.1 | custom fusion | bytes 1478400 | tf_op jit(solution)/shard_map/jit(_take)/gather | solution.py:27
  73.2 6.7 %fusion = f32[384,1920]{1,0:T(8,128)} fusion(bf16[1920,960]{0,1:T(8,128)(2,1)} %param.8, bf16[1920,960]{0,1:T(8,128)(2,1)} %param.9, bf16[960,384]{1,0:T(8,128)(2,1)S(1)} %gather_fusion.1, pred[960]{0:T(1024)(128)(4,1)S(1)} %compare_and_fusion.1), kind=kOutput, calls=%fused_computation.3 | convolution fusion | flops 1423319040 | bytes 11060160 | tf_op jit(solution)/shard_map/dot_general | solution.py:29
  79.9 0.0 all-reduce.2.cloned.1.call-update
  79.9 0.0 reduce-scatter.4.cloned.1.call-start
  80.0 89.5 %all-reduce.2.cloned.1.call-done = f32[384,1920]{1,0:T(8,128)} async-done(((f32[384,1920]{1,0:T(8,128)}), f32[384,1920]{1,0:T(8,128)}) %all-reduce.2.cloned.1.call-update) | async-done | bytes 2949136 | tf_op jit(solution)/shard_map/psum | solution.py:32
  169.5 3.1 %fusion.2 = f32[128,384]{0,1:T(8,128)S(1)} fusion(bf16[1920,128]{1,0:T(8,128)(2,1)S(1)} %copy-done, f32[384,1920]{1,0:T(8,128)} %all-reduce.2.cloned.1.call-done, f32[1920]{0:T(1024)S(1)} %copy-done.3), kind=kOutput, calls=%fused_computation.7 | convolution fusion | flops 193167360 | bytes 3644928 | tf_op jit(solution)/shard_map/dot_general | solution.py:36
  172.5 0.8 copy.27
  173.3 0.0 reduce-scatter.4.cloned.1.call-update
  173.4 30.0 %reduce-scatter.4.cloned.1.call-done = f32[16,384]{1,0:T(8,128)} async-done(((f32[128,384]{1,0:T(8,128)}), f32[16,384]{1,0:T(8,128)}) %reduce-scatter.4.cloned.1.call-update) | async-done | bytes 24592 | tf_op jit(solution)/shard_map/reduce_scatter | solution.py:35
  (14 shorter events, 0.1 us)
Async XLA Ops:
  6.5 162.9 %copy-start = (bf16[1920,128]{1,0:T(8,128)(2,1)S(1)}, bf16[1920,128]{1,0:T(8,128)(2,1)}, u32[]{:S(2)}) copy-start(bf16[1920,128]{1,0:T(8,128)(2,1)} %param.11) | copy-start | bytes 1474564
  6.5 23.9 %copy-start.1 = (f32[384,120]{0,1:T(8,128)S(1)}, f32[384,120]{0,1:T(8,128)}, u32[]{:S(2)}) copy-start(f32[384,120]{0,1:T(8,128)} %param.7) | copy-start | bytes 552964
  36.0 7.8 %copy-start.2 = (s32[960]{0:T(1024)S(1)}, s32[960]{0:T(1024)}, u32[]{:S(2)}) copy-start(s32[960]{0:T(1024)} %param.13) | copy-start | bytes 11524
  39.1 29.5 %all-to-all-start.1 = ((bf16[384,128,15]{0,2,1:T(8,128)(2,1)}), bf16[384,128,15]{0,2,1:T(8,128)(2,1)S(1)}, u32[]{:S(2)}, u32[]{:S(2)}) async-start(bf16[384,128,15]{0,2,1:T(8,128)(2,1)} %select_convert_fusion), calls=%async_computation.1 | async-start | bytes 3145728 | tf_op jit(solution)/shard_map/all_to_all | solution.py:19
  43.7 125.8 %all-reduce.2.cloned.1.call-start = ((), (), s32[]{:S(2)}) async-start(), calls=%async_computation.3 | async-start | bytes 5898240 | tf_op jit(solution)/shard_map/psum | solution.py:32
  79.9 89.6 %copy-start.3 = (f32[1920]{0:T(1024)S(1)}, f32[1920]{0:T(1024)}, u32[]{:S(2)}) copy-start(f32[1920]{0:T(1024)} %param.10) | copy-start | bytes 23044
  79.9 123.5 %reduce-scatter.4.cloned.1.call-start = ((), (), s32[]{:S(2)}) async-start(), calls=%async_computation.4 | async-start | bytes 221184 | tf_op jit(solution)/shard_map/reduce_scatter | solution.py:35
Sparse Core Ops, SparseCore 0:
  80.1 89.3 all-reduce.1
  173.5 29.8 reduce-scatter.3
where the time goes:
time: 211 us; the launch traced here: 210 us
  waiting for transfers between devices  144 us (68%)
  blocking collectives  20.5 us (10%)
  local copies, waits for them, and re-layouts  13.5 us (6%)
  between operations  13.5 us (6%)
  matrix products  9.77 us (5%)
  starting transfers between devices  4.72 us (2%)
  other arithmetic  3.98 us (2%)
    psum x1, waiting for transfers between devices, per_device(): totals = lax.psum(partial_value, 'ctg')  89.5 us
    reduce_scatter x1, waiting for transfers between devices, per_device(): lax.psum_scatter(lax.dot_general(columns, excess, (((0,), (1,)), ((), ())...  30 us
    all_to_all x1, waiting for transfers between devices, per_device(): lax.all_to_all(jnp.where(live_slot[None], values, 0.0).astype(jnp.bfloat1...  24.8 us
    all_to_all x1, blocking collectives, per_device(): lax.all_to_all(requests, ('ctg', 'line'), split_axis=0, concat_axis=0, ti...  20.5 us
    dot_general x1, matrix products, per_device(): lax.dot_general(outage_flow, weighted, (((1,), (1,)), ((), ())), preferre...  6.72 us
    gather x2, local copies, waits for them, and re-layouts, per_device(): values = jnp.take(base_flow, columns.reshape(-1), axis=1)  5.54 us
    all_to_all x1, starting transfers between devices, per_device(): lax.all_to_all(jnp.where(live_slot[None], values, 0.0).astype(jnp.bfloat1...  4.64 us
  transfers between devices with their start and end apart: 3, of which 3 were waited for; matrix products, arithmetic and copies ran while one was open for 0% of the time, Pallas kernels for 0%

commit v1 on v0

v1 whole, which is shorter than its diff:
```python
import jax
import jax.numpy as jnp
from jax import lax
from jax.experimental import pallas as pl
from jax.experimental.pallas import tpu as pltpu
from jax.sharding import PartitionSpec as P

MESH = pl.DeviceIdType.MESH
BF = jnp.bfloat16
F32 = jnp.float32
Q = 384
QH = 192
KD = 960
ML = 1920
MP = 2048
N_SEM = 176


def mod4(v):
    return lax.rem(v + 4, 4)


def kernel(
    fr_h, slot_h, base_h, lodf_h, dual_h, rating_h, sens_h, out_ref,
    fr_v, slot_v, base_v, base_b, lodf_v, dual_v, rating_v, sens_v, w_v,
    ask_s, ask_r, val_s, slots, of_acc, of_b,
    s1, own1, ro1, r1, s2, ro2, r2, ex, cut_acc, cut_v, fin_r,
    load_sem, send_sem, recv_sem,
):
    ctg = lax.axis_index("ctg")
    line = lax.axis_index("line")
    y, x = lax.div(ctg, 4), lax.rem(ctg, 4)
    z, core = lax.div(line, 2), lax.rem(line, 2)
    sent = []

    def device(dy=0, dx=0, dz=0, sibling=False):
        k = 1 - core if sibling else core
        return (mod4(y + dy) * 4 + mod4(x + dx), mod4(z + dz) * 2 + k)

    def send(src, dst, to, now=True):
        i = len(sent)
        copy = pltpu.make_async_remote_copy(
            src_ref=src, dst_ref=dst, send_sem=send_sem.at[i], recv_sem=recv_sem.at[i],
            device_id=to, device_id_type=MESH,
        )
        sent.append(copy)
        copy.start()
        return copy

    loads = {}
    plan = [("fr", fr_h, fr_v.at[0:15]), ("base", base_h, base_v), ("slot", slot_h, slot_v),
            ("lodf", lodf_h, lodf_v), ("dual", dual_h, dual_v), ("sens", sens_h, sens_v.at[0:ML]),
            ("rating", rating_h, rating_v.at[0:15])]
    for i, (name, src, dst) in enumerate(plan):
        loads[name] = pltpu.make_async_copy(src, dst, load_sem.at[i])
        loads[name].start()

    barrier = pltpu.get_barrier_semaphore()
    for s in range(1, 16):
        pl.semaphore_signal(barrier, inc=1, device_id=(lax.rem(ctg + s, 16), line), device_id_type=MESH)
    for s in range(1, 8):
        pl.semaphore_signal(barrier, inc=1, device_id=(ctg, lax.rem(line + s, 8)), device_id_type=MESH)

    loads["fr"].wait()
    row16 = lax.broadcasted_iota(jnp.int32, (16, 128), 0)
    lane16 = lax.broadcasted_iota(jnp.int32, (16, 128), 1)
    table = jnp.where(row16 < 15, fr_v[...], -1).astype(F32)
    ones = jnp.ones((128, 128), BF)
    for c in range(16):
        ask_s[c * 16 : c * 16 + 16, :] = jnp.where(lane16 == c * 8 + line, table, 0.0).astype(BF)
    ask_s[...] = jnp.dot(ask_s[...], ones, preferred_element_type=F32).astype(BF)
    mine = pl.ds(pl.multiple_of(ctg * 16, 16), 16)
    ask_r[mine, :] = ask_s[mine, :]
    pl.semaphore_wait(barrier, 22)
    asks = []
    for s in range(1, 16):
        p = lax.rem(ctg + s, 16)
        theirs = pl.ds(pl.multiple_of(p * 16, 16), 16)
        asks.append(send(ask_s.at[theirs, :], ask_r.at[mine, :], (p, line)))

    loads["base"].wait()
    base_b[0:112, :] = base_v[0:112, :].astype(BF)
    tail = jnp.concatenate([base_v[112:120, :], jnp.zeros((8, Q), F32)], axis=0)
    base_b[112:128, :] = tail.astype(BF)

    for a in asks:
        a.wait_recv()
    lane = lax.broadcasted_iota(jnp.int32, (256, 128), 1)
    pick = jnp.where(ask_r[...].astype(jnp.int32) == lane, 1.0, 0.0).astype(BF)
    val_s[...] = jnp.dot(pick, base_b[...], preferred_element_type=F32).astype(BF)
    vals = []
    for s in range(1, 16):
        p = lax.rem(ctg + s, 16)
        theirs = pl.ds(pl.multiple_of(p * 16, 16), 16)
        vals.append(send(val_s.at[theirs, :], slots.at[0, mine, :], (p, line)))
    slots[0, mine, :] = val_s[mine, :]

    loads["slot"].wait()
    sl = slot_v[...]
    o = lax.shift_right_logical(sl * 4370, 16)
    j = sl - o * 15
    lo = o & 7
    rel = (lax.shift_right_logical(lo, 1) - z + 4) & 3
    other = (lo & 1) ^ core
    place = (rel * 2 + other) * 256 + lax.shift_right_logical(o, 3) * 16 + j
    loads["lodf"].wait()
    loads["dual"].wait()

    def weigh(i, _):
        rows = pl.ds(pl.multiple_of(i * 32, 32), 32)
        w_v[rows, 0:ML] = (dual_v[rows, :].astype(F32) * lodf_v[rows, :].astype(F32)).astype(BF)
        w_v[rows, ML:MP] = jnp.zeros((32, MP - ML), BF)
        return 0

    lax.fori_loop(0, KD // 32, weigh, 0)
    loads["sens"].wait()
    sens_v[ML:MP, :] = jnp.zeros((MP - ML, 128), BF)
    loads["rating"].wait()

    for v in vals:
        v.wait_recv()

    up, down, sib = device(dz=1), device(dz=-1), device(sibling=True)
    a_up = send(slots.at[0], slots.at[6], up)
    a_down = send(slots.at[0], slots.at[2], down)
    a_sib = send(slots.at[0], slots.at[1], sib)

    row256 = lax.broadcasted_iota(jnp.int32, (256, KD), 0)

    def collect(block, first=False):
        hot = jnp.where(row256 == place - block * 256, 1.0, 0.0).astype(BF)
        part = lax.dot_general(slots[block], hot, (((0,), (0,)), ((), ())), preferred_element_type=F32)
        of_acc[...] = part if first else of_acc[...] + part

    collect(0, first=True)
    a_up.wait_recv()
    f_up = send(slots.at[6, 0:128], slots.at[4, 0:128], up)
    g6 = send(slots.at[6], slots.at[7], sib)
    a_down.wait_recv()
    f_down = send(slots.at[2, 128:256], slots.at[4, 128:256], down)
    g2 = send(slots.at[2], slots.at[3], sib)
    a_sib.wait_recv()
    collect(1)
    collect(6)
    collect(2)
    g6.wait_recv()
    collect(7)
    g2.wait_recv()
    collect(3)
    f_up.wait_recv()
    g4a = send(slots.at[4, 0:128], slots.at[5, 0:128], sib)
    f_down.wait_recv()
    g4b = send(slots.at[4, 128:256], slots.at[5, 128:256], sib)
    collect(4)
    g4a.wait_recv()
    g4b.wait_recv()
    collect(5)
    of_b[...] = of_acc[...].astype(BF)

    def product(h, d, i):
        a, b = (i, d) if h == 0 else (d, i)
        t = mod4(y + a) * 4 + mod4(x + b)
        cols = pl.ds(pl.multiple_of(t * 128, 128), 128)
        return jnp.dot(of_b[h * QH : (h + 1) * QH, :], w_v[:, cols], preferred_element_type=F32)

    def products(h, d):
        def step(i, _):
            s1[h, d, i] = product(h, d, i).astype(BF)
            return 0

        lax.fori_loop(0, 4, step, 0)

    def along(h, stage, d):
        return device(dx=d) if h == stage else device(dy=d)

    opp = [None, None]
    direct = [None, None]
    for h in range(2):
        products(h, 2)
        opp[h] = (send(s1.at[h, 2, 0:2], ro1.at[h, 0], along(h, 0, 1)),
                  send(s1.at[h, 2, 2:4], ro1.at[h, 1], along(h, 0, -1)))
    for h in range(2):
        products(h, 1)
        products(h, 3)
        direct[h] = (send(s1.at[h, 1, 2:4], r1.at[h, 0, 2:4], along(h, 0, 1)),
                     send(s1.at[h, 3, 0:2], r1.at[h, 1, 0:2], along(h, 0, -1)))
    merged = [None, None]
    for h in range(2):
        opp[h][0].wait_recv()
        s1[h, 1, 0:2] = (s1[h, 1, 0:2].astype(F32) + ro1[h, 0].astype(F32)).astype(BF)
        m0 = send(s1.at[h, 1, 0:2], r1.at[h, 0, 0:2], along(h, 0, 1))
        opp[h][1].wait_recv()
        s1[h, 3, 2:4] = (s1[h, 3, 2:4].astype(F32) + ro1[h, 1].astype(F32)).astype(BF)
        m1 = send(s1.at[h, 3, 2:4], r1.at[h, 1, 2:4], along(h, 0, -1))
        merged[h] = (m0, m1)
    for h in range(2):
        def own(i, _):
            own1[h, i] = product(h, 0, i)
            return 0

        lax.fori_loop(0, 4, own, 0)
    HH = QH // 2
    opp2 = [None, None]
    direct2 = [None, None]
    for h in range(2):
        for c in direct[h] + merged[h]:
            c.wait_recv()
        for i in (2, 1, 3):
            s2[h, i] = (own1[h, i] + r1[h, 0, i].astype(F32) + r1[h, 1, i].astype(F32)).astype(BF)
            if i == 2:
                opp2[h] = (send(s2.at[h, 2, 0:HH], ro2.at[h, 0], along(h, 1, 1)),
                           send(s2.at[h, 2, HH:QH], ro2.at[h, 1], along(h, 1, -1)))
        direct2[h] = (send(s2.at[h, 1, HH:QH], r2.at[h, 0, HH:QH], along(h, 1, 1)),
                      send(s2.at[h, 3, 0:HH], r2.at[h, 1, 0:HH], along(h, 1, -1)))
    merged2 = [None, None]
    for h in range(2):
        opp2[h][0].wait_recv()
        s2[h, 1, 0:HH] = (s2[h, 1, 0:HH].astype(F32) + ro2[h, 0].astype(F32)).astype(BF)
        m0 = send(s2.at[h, 1, 0:HH], r2.at[h, 0, 0:HH], along(h, 1, 1))
        opp2[h][1].wait_recv()
        s2[h, 3, HH:QH] = (s2[h, 3, HH:QH].astype(F32) + ro2[h, 1].astype(F32)).astype(BF)
        m1 = send(s2.at[h, 3, HH:QH], r2.at[h, 1, HH:QH], along(h, 1, -1))
        merged2[h] = (m0, m1)

    rows_r = lax.broadcasted_iota(jnp.int32, (16, 128), 0)
    limit = jnp.sum(jnp.where((rows_r == ctg) & (rows_r < 15), rating_v[...], 0.0), axis=0, keepdims=True)
    near1 = [None, None]
    near2 = [{}, {}]
    for h in range(2):
        for c in direct2[h] + merged2[h]:
            c.wait_recv()
        total = own1[h, 0] + own_sum(r1, h) + r2[h, 0].astype(F32) + r2[h, 1].astype(F32)
        ex[h, 0, 0] = (total - jnp.clip(total, -limit, limit)).astype(BF)
        near1[h] = (send(ex.at[h, 0, 0], ex.at[h, 0, 3], along(h, 1, 1)),
                    send(ex.at[h, 0, 0], ex.at[h, 0, 1], along(h, 1, -1)))

    def spread(h, i):
        near2[h][i] = (send(ex.at[h, 0, i], ex.at[h, 3, i], along(h, 0, 1)),
                       send(ex.at[h, 0, i], ex.at[h, 1, i], along(h, 0, -1)))

    def absorb(h, d, i, first=False):
        a, b = (i, d) if h == 0 else (d, i)
        t = mod4(y + a) * 4 + mod4(x + b)
        rows = pl.ds(pl.multiple_of(t * 128, 128), 128)
        part = jnp.dot(ex[h, d, i], sens_v[rows, :], preferred_element_type=F32)
        cut_acc[h] = part if first else cut_acc[h] + part

    far1 = [None, None]
    far2 = [{}, {}]
    for h in range(2):
        spread(h, 0)
        absorb(h, 0, 0, first=True)
    for h in range(2):
        near1[h][0].wait_recv()
        f0 = send(ex.at[h, 0, 3, 0:HH], ex.at[h, 0, 2, 0:HH], along(h, 1, 1))
        near1[h][1].wait_recv()
        f1 = send(ex.at[h, 0, 1, HH:QH], ex.at[h, 0, 2, HH:QH], along(h, 1, -1))
        far1[h] = (f0, f1)
        spread(h, 3)
        spread(h, 1)
        absorb(h, 0, 3)
        absorb(h, 0, 1)
    def pass_on(h, i):
        near2[h][i][0].wait_recv()
        if i < 2:
            far2[h][i] = send(ex.at[h, 3, i], ex.at[h, 2, i], along(h, 0, 1))
        near2[h][i][1].wait_recv()
        if i >= 2:
            far2[h][i] = send(ex.at[h, 1, i], ex.at[h, 2, i], along(h, 0, -1))
        absorb(h, 3, i)
        absorb(h, 1, i)

    for h in range(2):
        pass_on(h, 0)
    for h in range(2):
        far1[h][0].wait_recv()
        far1[h][1].wait_recv()
        spread(h, 2)
        absorb(h, 0, 2)
    for i in (1, 3, 2):
        for h in range(2):
            pass_on(h, i)
    for i in (0, 1, 3, 2):
        for h in range(2):
            far2[h][i].wait_recv()
            absorb(h, 2, i)

    for h in range(2):
        cut_v[h * QH : (h + 1) * QH, :] = cut_acc[h]
    flipped = [cut_v[i * 128 : (i + 1) * 128, :].T for i in range(3)]
    for i in range(3):
        cut_t = flipped[i]
        for p in range(8):
            fin_r[8 + p, :, i * 128 : (i + 1) * 128] = cut_t[p * 16 : (p + 1) * 16, :]
    fins = []
    for s in range(1, 8):
        p = lax.rem(line + s, 8)
        fins.append(send(fin_r.at[8 + p], fin_r.at[s], (ctg, p)))
    total = fin_r[8 + line]
    for s, f in enumerate(fins):
        f.wait_recv()
        total = total + fin_r[s + 1]
    out_ref[...] = total
    for c in sent:
        c.wait_send()


def own_sum(r1, h):
    return r1[h, 0, 0].astype(F32) + r1[h, 1, 0].astype(F32)


def per_device(base_flow, lodf, dual, rating, sens, fetch_rows, ctg_slot):
    hbm = pl.BlockSpec(memory_space=pl.ANY)
    vm = pltpu.VMEM
    return pl.pallas_call(
        kernel,
        out_shape=jax.ShapeDtypeStruct((16, Q), F32),
        in_specs=[hbm] * 7,
        out_specs=pl.BlockSpec(memory_space=pltpu.VMEM),
        scratch_shapes=[
            vm((16, 128), jnp.int32), vm((1, KD), jnp.int32), vm((120, Q), F32), vm((128, Q), BF),
            vm((KD, ML), BF), vm((KD, ML), BF), vm((16, 128), F32), vm((MP, 128), BF), vm((KD, MP), BF),
            vm((256, 128), BF), vm((256, 128), BF), vm((256, Q), BF), vm((8, 256, Q), BF),
            vm((Q, KD), F32), vm((Q, KD), BF),
            vm((2, 4, 4, QH, 128), BF), vm((2, 4, QH, 128), F32), vm((2, 2, 2, QH, 128), BF), vm((2, 2, 4, QH, 128), BF),
            vm((2, 4, QH, 128), BF), vm((2, 2, QH // 2, 128), BF), vm((2, 2, QH, 128), BF),
            vm((2, 4, 4, QH, 128), BF), vm((2, QH, 128), F32), vm((Q, 128), F32), vm((16, 16, Q), F32),
            pltpu.SemaphoreType.DMA((8,)), pltpu.SemaphoreType.DMA((N_SEM,)), pltpu.SemaphoreType.DMA((N_SEM,)),
        ],
        compiler_params=pltpu.CompilerParams(
            collective_id=0, has_side_effects=True, vmem_limit_bytes=56 * 1024 * 1024
        ),
    )(fetch_rows[0].T, ctg_slot[None, :], base_flow.T, lodf.T, dual.T, rating.reshape(15, 128), sens)


def solution(mesh):
    in_specs = (
        P(None, ("ctg", "line")),
        P("line", "ctg"),
        P("line", "ctg"),
        P("line"),
        P("line", "ctg"),
        P("ctg", None, None),
        P("ctg"),
    )
    out_specs = P(("ctg", "line"), None)
    return jax.shard_map(
        per_device, mesh=mesh, in_specs=in_specs, out_specs=out_specs, check_vma=False
    )
```

time: 211 us -> 75.1 us (0.36)
  waiting for transfers between devices: 144 us -> 0 us
  Pallas kernels: 0 us -> 71.3 us
  blocking collectives: 20.5 us -> 0 us
  between operations: 13.5 us -> 0.01 us
  local copies, waits for them, and re-layouts: 13.5 us -> 2.64 us
  matrix products: 9.77 us -> 0 us
  starting transfers between devices: 4.72 us -> 0 us
  other arithmetic: 3.98 us -> 0 us
    psum x1 -> x0, waiting for transfers between devices: 89.5 us -> none  [per_device(): totals = lax.psum(partial_value, 'ctg')]
    pallas_call x0 -> x1, Pallas kernels: none -> 71.3 us  [per_device(): pl.pallas_call(kernel, out_shape=jax.ShapeDtypeStruct((16, Q), F32), in_s...]
    reduce_scatter x1 -> x0, waiting for transfers between devices: 30 us -> none  [per_device(): lax.psum_scatter(lax.dot_general(columns, excess, (((0,), (1,)), ((), ())...]
    all_to_all x1 -> x0, waiting for transfers between devices: 24.8 us -> none  [per_device(): lax.all_to_all(jnp.where(live_slot[None], values, 0.0).astype(jnp.bfloat1...]
    all_to_all x1 -> x0, blocking collectives: 20.5 us -> none  [per_device(): lax.all_to_all(requests, ('ctg', 'line'), split_axis=0, concat_axis=0, ti...]
    dot_general x2 -> x0, matrix products: 9.77 us -> none  [the longest x1 6.72 us: per_device(): lax.dot_general(outage_flow, weighted, (((1,), (1,)), ((), ())), preferre...]
    gather x3 -> x0, local copies, waits for them, and re-layouts: 9.65 us -> none  [the longest x2 5.54 us: per_device(): values = jnp.take(base_flow, columns.reshape(-1), axis=1)]
    all_to_all x1 -> x0, starting transfers between devices: 4.64 us -> none  [per_device(): lax.all_to_all(jnp.where(live_slot[None], values, 0.0).astype(jnp.bfloat1...]
  transfers between devices with their start and end apart: 3 -> 0, of which waited for: 3 -> 0; matrix products, arithmetic and copies ran while one was open for 0% -> 0% of each run, Pallas kernels for 0% -> 0%
where the time goes in v1:
time: 75.1 us; the launch traced here: 73.9 us
  Pallas kernels  71.3 us (95%)
  local copies, waits for them, and re-layouts  2.64 us (4%)
    pallas_call x1, Pallas kernels, per_device(): pl.pallas_call(kernel, out_shape=jax.ShapeDtypeStruct((16, Q), F32), in_s...  71.3 us
    unnamed x2, local copies, waits for them, and re-layouts  2.64 us

profile of v1, /device:TPU:0, one launch (start us, length us, event | category | flops | bytes accessed | tf_op | source)
XLA Modules:
  0.0 73.9 jit_solution(16431038499762086676)
XLA Ops:
  0.0 1.3 %copy.10 = s32[1,128,15]{1,2,0:T(8,128)} copy(s32[1,128,15]{1,0,2:T(1,128)} %param.12) | data formatting | bytes 15360
  1.3 71.3 %shard_map.73 = f32[16,384]{1,0:T(8,128)} custom-call(s32[15,128]{1,0:T(8,128)} %bitcast.13, s32[1,960]{1,0:T(1,128)} %bitcast.15, f32[120,384]{1,0:T(8,128)} %bitcast.12, bf16[960,1920]{1,0:T(8,128)(2,1)} %bitcast.10, bf16[960,1920]{1,0:T(8,128)(2,1)} %bitcast.11, f32[15,128]{1,0:T(8,128)} %bitcast.14, bf16[1920,128]{1,0:T(8,128)(2,1)} %sens_h.1), custom_call_target="tpu_custom_call" | custom-call | tf_op jit(solution)/shard_map/pallas_call | solution.py:315
  72.6 1.3 %copy.12 = f32[16,384]{1,0:T(8,128)} copy(f32[16,384]{1,0:T(8,128)} %shard_map.73) | data formatting | bytes 49152

commit v2 on v0

v2 whole, which is shorter than its diff:
```python
import jax
import jax.numpy as jnp
from jax import lax
from jax.experimental import pallas as pl
from jax.experimental.pallas import tpu as pltpu
from jax.sharding import PartitionSpec as P

MESH = pl.DeviceIdType.MESH
BF = jnp.bfloat16
F32 = jnp.float32
Q = 384
NC = 3
HR = 64
KD = 960
ML = 1920
MP = 2048
N_SEM = 144


def mod4(v):
    return lax.rem(v + 4, 4)


def at128(i):
    return pl.ds(pl.multiple_of(i * 128, 128), 128)


def kernel(
    fr_h, slot_h, base_h, lodf_h, dual_h, rating_h, sens_h, out_ref,
    fr_v, slot_v, base_v, base_b, lodf_v, dual_v, rating_v, sens_v, sens_x, w_v, hot,
    ask_s, ask_r, val_s, slots, of_b,
    s1, r1, t2, s2, r2, ex, part, kr, u_v, zs, zr, v_v, rr,
    load_sem, send_sem, recv_sem,
):
    ctg = lax.axis_index("ctg")
    line = lax.axis_index("line")
    y, x = lax.div(ctg, 4), lax.rem(ctg, 4)
    z, core = lax.div(line, 2), lax.rem(line, 2)
    here = (x, y)
    sent = []

    def send(src, dst, to):
        i = len(sent)
        copy = pltpu.make_async_remote_copy(
            src_ref=src, dst_ref=dst, send_sem=send_sem.at[i], recv_sem=recv_sem.at[i],
            device_id=to, device_id_type=MESH,
        )
        sent.append(copy)
        copy.start()
        return copy

    def along(axis, d):
        return (y * 4 + mod4(x + d), line) if axis == 0 else (mod4(y + d) * 4 + x, line)

    sib = (ctg, z * 2 + 1 - core)

    loads = {}
    plan = [("fr", fr_h, fr_v.at[0:15]), ("base", base_h, base_v), ("slot", slot_h, slot_v),
            ("lodf", lodf_h, lodf_v), ("dual", dual_h, dual_v),
            ("sens0", sens_h.at[0:4], sens_v.at[0]), ("sens1", sens_h.at[4:8], sens_v.at[1]),
            ("sens2", sens_h.at[8:12], sens_v.at[2]), ("sens3", sens_h.at[12:15], sens_v.at[3, 0:3]),
            ("rating", rating_h, rating_v.at[0:15])]
    for i, (name, src, dst) in enumerate(plan):
        loads[name] = pltpu.make_async_copy(src, dst, load_sem.at[i])
        loads[name].start()

    barrier = pltpu.get_barrier_semaphore()
    for s in range(1, 16):
        pl.semaphore_signal(barrier, inc=1, device_id=(lax.rem(ctg + s, 16), line), device_id_type=MESH)
    for e in range(1, 4):
        pl.semaphore_signal(barrier, inc=1, device_id=(ctg, mod4(z + e) * 2 + core), device_id_type=MESH)
    pl.semaphore_signal(barrier, inc=1, device_id=sib, device_id_type=MESH)

    loads["fr"].wait()
    row16 = lax.broadcasted_iota(jnp.int32, (16, 128), 0)
    lane16 = lax.broadcasted_iota(jnp.int32, (16, 128), 1)
    fr_v[15] = jnp.full((1, 128), -1, jnp.int32)
    table = fr_v[...].reshape(16, 128).astype(F32)
    ones = jnp.ones((128, 128), BF)
    for c in range(16):
        ask_s[c * 16 : c * 16 + 16, :] = jnp.where(lane16 == c * 8 + line, table, 0.0).astype(BF)
    ask_s[...] = jnp.dot(ask_s[...], ones, preferred_element_type=F32).astype(BF)
    mine = pl.ds(pl.multiple_of(ctg * 16, 16), 16)
    ask_r[mine, :] = ask_s[mine, :]
    pl.semaphore_wait(barrier, 19)
    asks = []
    for s in range(1, 16):
        p = lax.rem(ctg + s, 16)
        theirs = pl.ds(pl.multiple_of(p * 16, 16), 16)
        asks.append(send(ask_s.at[theirs, :], ask_r.at[mine, :], (p, line)))

    loads["base"].wait()
    base_b[0:112, :] = base_v[0:112, :].astype(BF)
    tail = jnp.concatenate([base_v[112:120, :], jnp.zeros((8, Q), F32)], axis=0)
    base_b[112:128, :] = tail.astype(BF)
    loads["slot"].wait()
    sl = slot_v[...]
    o = lax.shift_right_logical(sl * 4370, 16)
    lo = o & 7
    rel = (z - lax.shift_right_logical(lo, 1) + 4) & 3
    other = (lo & 1) ^ core
    place = (other * 4 + rel) * 256 + lax.shift_right_logical(o, 3) * 16 + (sl - o * 15)
    row256 = lax.broadcasted_iota(jnp.int32, (256, KD), 0)

    def heat(b, _):
        hot[pl.ds(pl.multiple_of(b * 256, 256), 256), :] = jnp.where(row256 == place - b * 256, 1.0, 0.0).astype(BF)
        return 0

    lax.fori_loop(0, 8, heat, 0)

    for a in asks:
        a.wait_recv()
    lane = lax.broadcasted_iota(jnp.int32, (256, 128), 1)
    pick = jnp.where(ask_r[...].astype(jnp.int32) == lane, 1.0, 0.0).astype(BF)
    found = jnp.dot(pick, base_b[...], preferred_element_type=F32).astype(BF)
    for i in range(NC):
        val_s[i] = found[:, i * 128 : (i + 1) * 128]
    vals = []
    for s in range(1, 16):
        p = lax.rem(ctg + s, 16)
        theirs = pl.ds(pl.multiple_of(p * 16, 16), 16)
        vals.append(send(val_s.at[:, theirs, :], slots.at[:, 0, mine, :], (p, line)))
    for i in range(NC):
        slots[i, 0, mine, :] = val_s[i, mine, :]

    for name in ("sens0", "sens1", "sens2", "sens3"):
        loads[name].wait()
    sens_v[3, 3] = jnp.zeros((128, 128), BF)
    sens_x[0, :, :, 0:128] = sens_v[y]
    sens_x[1, :, :, 0:128] = sens_v[:, x]
    loads["lodf"].wait()
    loads["dual"].wait()

    def weigh(i, _):
        rows = pl.ds(pl.multiple_of(i * 32, 32), 32)
        w_v[rows, 0:ML] = (dual_v[rows, :].astype(F32) * lodf_v[rows, :].astype(F32)).astype(BF)
        w_v[rows, ML:MP] = jnp.zeros((32, MP - ML), BF)
        return 0

    lax.fori_loop(0, KD // 32, weigh, 0)
    loads["rating"].wait()
    rows_r = lax.broadcasted_iota(jnp.int32, (16, 128), 0)
    limit = jnp.sum(jnp.where((rows_r == ctg) & (rows_r < 15), rating_v[...], 0.0), axis=0, keepdims=True)

    for v in vals:
        v.wait_recv()

    far, near, relayed = [None] * NC, [None] * NC, [None] * NC

    def gather(i):
        far[i] = [send(slots.at[i, 0], slots.at[i, e], (ctg, mod4(z + e) * 2 + core)) for e in (2, 1, 3)]
        near[i] = send(slots.at[i, 0], slots.at[i, 4], sib)

    def relay(i):
        for c in far[i]:
            c.wait_recv()
        relayed[i] = send(slots.at[i, 1:4], slots.at[i, 5:8], sib)

    def collect(i):
        tn = (((0,), (0,)), ((), ()))
        a = lax.dot_general(slots[i, 0:4].reshape(1024, 128), hot[0:1024, :], tn, preferred_element_type=F32)
        near[i].wait_recv()
        relayed[i].wait_recv()
        b = lax.dot_general(slots[i, 4:8].reshape(1024, 128), hot[1024:2048, :], tn, preferred_element_type=F32)
        of_b[i] = (a + b).astype(BF)

    sum1, sum2 = [[[], []] for _ in range(NC)], [[[], []] for _ in range(NC)]

    def shifts(i):
        for e in (2, 1, 3, 0):
            g = mod4(y + e)
            cols = pl.ds(pl.multiple_of(g * 512, 512), 512)
            got = jnp.dot(of_b[i], w_v[:, cols], preferred_element_type=F32).astype(BF)
            for t in range(4):
                tile = got[:, t * 128 : (t + 1) * 128]
                s1[i, 0, t, g] = tile[0:HR]
                s1[i, 1, g, t] = tile[HR:128]
            if e:
                sum1[i][1].append(send(s1.at[i, 1, g], r1.at[i, 1, e - 1], along(1, e)))
        for e in (2, 1, 3):
            sum1[i][0].append(send(s1.at[i, 0, mod4(x + e)], r1.at[i, 0, e - 1], along(0, e)))

    def second(i):
        for h in (1, 0):
            for c in sum1[i][h]:
                c.wait_recv()
            total = s1[i, h, here[h]].astype(F32)
            for e in range(3):
                total = total + r1[i, h, e].astype(F32)
            t2[i, h] = total
            s2[i, h] = total.astype(BF)
            for e in (2, 1, 3):
                sum2[i][h].append(
                    send(s2.at[i, h, mod4(here[1 - h] + e)], r2.at[i, h, e - 1], along(1 - h, e)))

    gathered = [[[], []] for _ in range(NC)]

    def excess(i):
        for h in (1, 0):
            for c in sum2[i][h]:
                c.wait_recv()
            total = t2[i, h, here[1 - h]]
            for e in range(3):
                total = total + r2[i, h, e].astype(F32)
            lanes = at128(here[h])
            ex[i, h, :, lanes] = (total - jnp.clip(total, -limit, limit)).astype(BF)
            for e in (2, 1, 3):
                gathered[i][h].append(send(ex.at[i, h, :, lanes], ex.at[i, h, :, lanes], along(h, e)))

    crossed, zsum, last = [None] * NC, [None] * NC, [[] for _ in range(NC)]

    def cut(i):
        both = []
        for h in range(2):
            for c in gathered[i][h]:
                c.wait_recv()
            both.append(jnp.dot(ex[i, h], sens_x[h].reshape(512, 512), preferred_element_type=F32))
        both = jnp.concatenate(both, axis=0)
        for e in range(4):
            part[i, e] = both[:, e * 128 : (e + 1) * 128].T.reshape(4, 2, 16, 128)
        crossed[i] = send(part.at[i, :, :, 1 - core], kr.at[i], sib)

    def cut_z(i):
        crossed[i].wait_recv()
        total = part[i, :, :, core] + kr[i]
        u_v[i] = total
        zs[i] = total.astype(BF)
        zsum[i] = [send(zs.at[i, :, mod4(z + e)], zr.at[i, e - 1], (ctg, mod4(z + e) * 2 + core)) for e in (2, 1, 3)]

    def cut_last(i):
        for c in zsum[i]:
            c.wait_recv()
        total = u_v[i, :, z]
        for e in range(3):
            total = total + zr[i, e].astype(F32)
        v_v[i] = total
        for h in range(2):
            for e in (2, 1, 3):
                last[i].append(send(v_v.at[i, e], rr.at[i, h, e - 1], along(1 - h, -e)))

    def finish(i):
        for c in last[i]:
            c.wait_recv()
        lane_o = lax.broadcasted_iota(jnp.int32, (16, 128), 1)
        total = v_v[i, 0]
        for e in range(3):
            total = total + jnp.where(lane_o < HR, rr[i, 0, e], rr[i, 1, e])
        out_ref[:, i * 128 : (i + 1) * 128] = total

    for i in range(NC):
        gather(i)
    swaps = []
    for e in (2, 1, 3):
        swaps.append(send(sens_v.at[mod4(y + e)], sens_x.at[0, :, :, e * 128 : (e + 1) * 128], along(1, e)))
        swaps.append(send(sens_v.at[:, mod4(x + e)], sens_x.at[1, :, :, e * 128 : (e + 1) * 128], along(0, e)))
    relay(0)
    collect(0)
    shifts(0)
    relay(1)
    collect(1)
    shifts(1)
    relay(2)
    collect(2)
    second(0)
    shifts(2)
    second(1)
    excess(0)
    for c in swaps:
        c.wait_recv()
    second(2)
    excess(1)
    cut(0)
    excess(2)
    cut_z(0)
    cut(1)
    cut_z(1)
    cut_last(0)
    cut(2)
    cut_last(1)
    cut_z(2)
    cut_last(2)
    for i in range(NC):
        finish(i)
    for c in sent:
        c.wait_send()


def per_device(base_flow, lodf, dual, rating, sens, fetch_rows, ctg_slot):
    hbm = pl.BlockSpec(memory_space=pl.ANY)
    vm = pltpu.VMEM
    return pl.pallas_call(
        kernel,
        out_shape=jax.ShapeDtypeStruct((16, Q), F32),
        in_specs=[hbm] * 7,
        out_specs=pl.BlockSpec(memory_space=pltpu.VMEM),
        scratch_shapes=[
            vm((16, 1, 128), jnp.int32), vm((1, KD), jnp.int32), vm((120, Q), F32), vm((128, Q), BF),
            vm((KD, ML), BF), vm((KD, ML), BF), vm((16, 128), F32), vm((4, 4, 128, 128), BF), vm((2, 4, 128, 512), BF),
            vm((KD, MP), BF), vm((2048, KD), BF),
            vm((256, 128), BF), vm((256, 128), BF), vm((NC, 256, 128), BF), vm((NC, 8, 256, 128), BF), vm((NC, 128, KD), BF),
            vm((NC, 2, 4, 4, HR, 128), BF), vm((NC, 2, 3, 4, HR, 128), BF), vm((NC, 2, 4, HR, 128), F32),
            vm((NC, 2, 4, HR, 128), BF), vm((NC, 2, 3, HR, 128), BF), vm((NC, 2, HR, 512), BF),
            vm((NC, 4, 4, 2, 16, 128), F32), vm((NC, 4, 4, 16, 128), F32), vm((NC, 4, 4, 16, 128), F32),
            vm((NC, 4, 4, 16, 128), BF), vm((NC, 3, 4, 16, 128), BF), vm((NC, 4, 16, 128), F32), vm((NC, 2, 3, 16, 128), F32),
            pltpu.SemaphoreType.DMA((10,)), pltpu.SemaphoreType.DMA((N_SEM,)), pltpu.SemaphoreType.DMA((N_SEM,)),
        ],
        compiler_params=pltpu.CompilerParams(
            collective_id=0, has_side_effects=True, vmem_limit_bytes=56 * 1024 * 1024
        ),
    )(fetch_rows.transpose(2, 0, 1), ctg_slot[None, :], base_flow.T, lodf.T, dual.T, rating.reshape(15, 128),
      sens.reshape(15, 128, 128))


def solution(mesh):
    in_specs = (
        P(None, ("ctg", "line")),
        P("line", "ctg"),
        P("line", "ctg"),
        P("line"),
        P("line", "ctg"),
        P("ctg", None, None),
        P("ctg"),
    )
    out_specs = P(("ctg", "line"), None)
    return jax.shard_map(
        per_device, mesh=mesh, in_specs=in_specs, out_specs=out_specs, check_vma=False
    )
```

time: 211 us -> 59.9 us (0.28)
  waiting for transfers between devices: 144 us -> 0 us
  Pallas kernels: 0 us -> 58.4 us
  blocking collectives: 20.5 us -> 0 us
  between operations: 13.5 us -> 0.01 us
  local copies, waits for them, and re-layouts: 13.5 us -> 1.35 us
  matrix products: 9.77 us -> 0 us
  starting transfers between devices: 4.72 us -> 0 us
  other arithmetic: 3.98 us -> 0 us
    psum x1 -> x0, waiting for transfers between devices: 89.5 us -> none  [per_device(): totals = lax.psum(partial_value, 'ctg')]
    pallas_call x0 -> x1, Pallas kernels: none -> 58.4 us  [per_device(): pl.pallas_call(kernel, out_shape=jax.ShapeDtypeStruct((16, Q), F32), in_s...]
    reduce_scatter x1 -> x0, waiting for transfers between devices: 30 us -> none  [per_device(): lax.psum_scatter(lax.dot_general(columns, excess, (((0,), (1,)), ((), ())...]
    all_to_all x1 -> x0, waiting for transfers between devices: 24.8 us -> none  [per_device(): lax.all_to_all(jnp.where(live_slot[None], values, 0.0).astype(jnp.bfloat1...]
    all_to_all x1 -> x0, blocking collectives: 20.5 us -> none  [per_device(): lax.all_to_all(requests, ('ctg', 'line'), split_axis=0, concat_axis=0, ti...]
    dot_general x2 -> x0, matrix products: 9.77 us -> none  [the longest x1 6.72 us: per_device(): lax.dot_general(outage_flow, weighted, (((1,), (1,)), ((), ())), preferre...]
    gather x3 -> x0, local copies, waits for them, and re-layouts: 9.65 us -> none  [the longest x2 5.54 us: per_device(): values = jnp.take(base_flow, columns.reshape(-1), axis=1)]
    all_to_all x1 -> x0, starting transfers between devices: 4.64 us -> none  [per_device(): lax.all_to_all(jnp.where(live_slot[None], values, 0.0).astype(jnp.bfloat1...]
  transfers between devices with their start and end apart: 3 -> 0, of which waited for: 3 -> 0; matrix products, arithmetic and copies ran while one was open for 0% -> 0% of each run, Pallas kernels for 0% -> 0%
where the time goes in v2:
time: 59.9 us; the launch traced here: 59.7 us
  Pallas kernels  58.4 us (97%)
  local copies, waits for them, and re-layouts  1.35 us (2%)
    pallas_call x1, Pallas kernels, per_device(): pl.pallas_call(kernel, out_shape=jax.ShapeDtypeStruct((16, Q), F32), in_s...  58.4 us
    unnamed x1, local copies, waits for them, and re-layouts  1.35 us

profile of v2, /device:TPU:0, one launch (start us, length us, event | category | flops | bytes accessed | tf_op | source)
XLA Modules:
  0.0 59.7 jit_solution(14215421094440759990)
XLA Ops:
  0.0 58.4 %shard_map.73 = f32[16,384]{1,0:T(8,128)} custom-call(s32[15,1,128]{2,1,0:T(1,128)} %bitcast.12, s32[1,960]{1,0:T(1,128)} %bitcast.13, f32[120,384]{1,0:T(8,128)} %bitcast.10, bf16[960,1920]{1,0:T(8,128)(2,1)} %bitcast.7, bf16[960,1920]{1,0:T(8,128)(2,1)} %bitcast.8, f32[15,128]{1,0:T(8,128)} %bitcast.11, bf16[15,128,128]{2,1,0:T(8,128)(2,1)} %bitcast.9), custom_call_target="tpu_custom_call" | custom-call | tf_op jit(solution)/shard_map/pallas_call | solution.py:291
  58.4 1.3 %copy.9 = f32[16,384]{1,0:T(8,128)} copy(f32[16,384]{1,0:T(8,128)} %shard_map.73) | data formatting | bytes 49152

commit v3 on v2

--- a/solution.py
+++ b/solution.py
@@ -14,7 +14,7 @@
 KD = 960
 ML = 1920
 MP = 2048
-N_SEM = 144
+N_SEM = 160
 
 
 def mod4(v):
@@ -27,9 +27,9 @@
 
 def kernel(
     fr_h, slot_h, base_h, lodf_h, dual_h, rating_h, sens_h, out_ref,
-    fr_v, slot_v, base_v, base_b, lodf_v, dual_v, rating_v, sens_v, sens_x, w_v, hot,
-    ask_s, ask_r, val_s, slots, of_b,
-    s1, r1, t2, s2, r2, ex, part, kr, u_v, zs, zr, v_v, rr,
+    slot_v, base_v, base_b, lodf_v, dual_v, rating_v, sens_v, sens_x, w_v, hot,
+    ask_r, val_s, slots, of_b,
+    s1, r1, t2, s2, r2, ex, part, zs, zr, v_v, rr,
     load_sem, send_sem, recv_sem,
 ):
     ctg = lax.axis_index("ctg")
@@ -37,7 +37,7 @@
     y, x = lax.div(ctg, 4), lax.rem(ctg, 4)
     z, core = lax.div(line, 2), lax.rem(line, 2)
     here = (x, y)
-    sent = []
+    sent, ended = [], set()
 
     def send(src, dst, to):
         i = len(sent)
@@ -49,45 +49,41 @@
         copy.start()
         return copy
 
+    def drain(copies):
+        for c in copies:
+            if id(c) not in ended:
+                c.wait_send()
+                ended.add(id(c))
+
     def along(axis, d):
         return (y * 4 + mod4(x + d), line) if axis == 0 else (mod4(y + d) * 4 + x, line)
 
     sib = (ctg, z * 2 + 1 - core)
+    steps = sorted(((a, b) for a in range(4) for b in range(4) if a or b), key=lambda ab: -(min(ab[0], 4 - ab[0]) + min(ab[1], 4 - ab[1])))
+    peers = [mod4(y + a) * 4 + mod4(x + b) for a, b in steps]
 
     loads = {}
-    plan = [("fr", fr_h, fr_v.at[0:15]), ("base", base_h, base_v), ("slot", slot_h, slot_v),
+    plan = [("base", base_h, base_v), ("slot", slot_h, slot_v),
             ("lodf", lodf_h, lodf_v), ("dual", dual_h, dual_v),
             ("sens0", sens_h.at[0:4], sens_v.at[0]), ("sens1", sens_h.at[4:8], sens_v.at[1]),
             ("sens2", sens_h.at[8:12], sens_v.at[2]), ("sens3", sens_h.at[12:15], sens_v.at[3, 0:3]),
             ("rating", rating_h, rating_v.at[0:15])]
     for i, (name, src, dst) in enumerate(plan):
-        loads[name] = pltpu.make_async_copy(src, dst, load_sem.at[i])
+        loads[name] = pltpu.make_async_copy(src, dst, load_sem.at[i + 1])
         loads[name].start()
 
     barrier = pltpu.get_barrier_semaphore()
-    for s in range(1, 16):
-        pl.semaphore_signal(barrier, inc=1, device_id=(lax.rem(ctg + s, 16), line), device_id_type=MESH)
-    for e in range(1, 4):
-        pl.semaphore_signal(barrier, inc=1, device_id=(ctg, mod4(z + e) * 2 + core), device_id_type=MESH)
-    pl.semaphore_signal(barrier, inc=1, device_id=sib, device_id_type=MESH)
-
-    loads["fr"].wait()
-    row16 = lax.broadcasted_iota(jnp.int32, (16, 128), 0)
-    lane16 = lax.broadcasted_iota(jnp.int32, (16, 128), 1)
-    fr_v[15] = jnp.full((1, 128), -1, jnp.int32)
-    table = fr_v[...].reshape(16, 128).astype(F32)
-    ones = jnp.ones((128, 128), BF)
-    for c in range(16):
-        ask_s[c * 16 : c * 16 + 16, :] = jnp.where(lane16 == c * 8 + line, table, 0.0).astype(BF)
-    ask_s[...] = jnp.dot(ask_s[...], ones, preferred_element_type=F32).astype(BF)
+    for p in peers:
+        pl.semaphore_signal(barrier, inc=1, device_id=(p, line), device_id_type=MESH)
+    for e in range(1, 8):
+        pl.semaphore_signal(barrier, inc=1, device_id=(ctg, lax.rem(line + e, 8)), device_id_type=MESH)
+
     mine = pl.ds(pl.multiple_of(ctg * 16, 16), 16)
-    ask_r[mine, :] = ask_s[mine, :]
-    pl.semaphore_wait(barrier, 19)
-    asks = []
-    for s in range(1, 16):
-        p = lax.rem(ctg + s, 16)
-        theirs = pl.ds(pl.multiple_of(p * 16, 16), 16)
-        asks.append(send(ask_s.at[theirs, :], ask_r.at[mine, :], (p, line)))
+    pl.semaphore_wait(barrier, 22)
+    asks = [send(fr_h, ask_r.at[ctg, 0:15], (p, line)) for p in peers]
+    own_ask = pltpu.make_async_copy(fr_h, ask_r.at[ctg, 0:15], load_sem.at[0])
+    own_ask.start()
+    ask_r[:, 15:16] = jnp.full((16, 1, 1, 128), -1, jnp.int32)
 
     loads["base"].wait()
     base_b[0:112, :] = base_v[0:112, :].astype(BF)
@@ -110,14 +106,16 @@
 
     for a in asks:
         a.wait_recv()
+    own_ask.wait()
     lane = lax.broadcasted_iota(jnp.int32, (256, 128), 1)
-    pick = jnp.where(ask_r[...].astype(jnp.int32) == lane, 1.0, 0.0).astype(BF)
+    wanted = jnp.where(lane == ctg * 8 + line, ask_r[...].reshape(256, 128), 0).astype(BF)
+    wanted = jnp.dot(wanted, jnp.ones((128, 128), BF), preferred_element_type=F32)
+    pick = jnp.where(wanted == lane.astype(F32), 1.0, 0.0).astype(BF)
     found = jnp.dot(pick, base_b[...], preferred_element_type=F32).astype(BF)
     for i in range(NC):
         val_s[i] = found[:, i * 128 : (i + 1) * 128]
     vals = []
-    for s in range(1, 16):
-        p = lax.rem(ctg + s, 16)
+    for p in peers:
         theirs = pl.ds(pl.multiple_of(p * 16, 16), 16)
         vals.append(send(val_s.at[:, theirs, :], slots.at[:, 0, mine, :], (p, line)))
     for i in range(NC):
@@ -207,7 +205,7 @@
             for e in (2, 1, 3):
                 gathered[i][h].append(send(ex.at[i, h, :, lanes], ex.at[i, h, :, lanes], along(h, e)))
 
-    crossed, zsum, last = [None] * NC, [None] * NC, [[] for _ in range(NC)]
+    zsum, last = [None] * NC, [[] for _ in range(NC)]
 
     def cut(i):
         both = []
@@ -217,21 +215,19 @@
             both.append(jnp.dot(ex[i, h], sens_x[h].reshape(512, 512), preferred_element_type=F32))
         both = jnp.concatenate(both, axis=0)
         for e in range(4):
-            part[i, e] = both[:, e * 128 : (e + 1) * 128].T.reshape(4, 2, 16, 128)
-        crossed[i] = send(part.at[i, :, :, 1 - core], kr.at[i], sib)
-
-    def cut_z(i):
-        crossed[i].wait_recv()
-        total = part[i, :, :, core] + kr[i]
-        u_v[i] = total
-        zs[i] = total.astype(BF)
-        zsum[i] = [send(zs.at[i, :, mod4(z + e)], zr.at[i, e - 1], (ctg, mod4(z + e) * 2 + core)) for e in (2, 1, 3)]
+            flat = both[:, e * 128 : (e + 1) * 128].T.reshape(8, 16, 128)
+            part[i, e] = flat
+            zs[i, e] = flat.astype(BF)
+        zsum[i] = []
+        for e in (4, 5, 3, 2, 6, 7, 1):
+            p = lax.rem(line + e, 8)
+            zsum[i].append(send(zs.at[i, :, p], zr.at[i, e - 1], (ctg, p)))
 
     def cut_last(i):
         for c in zsum[i]:
             c.wait_recv()
-        total = u_v[i, :, z]
-        for e in range(3):
+        total = part[i, :, line]
+        for e in range(7):
             total = total + zr[i, e].astype(F32)
         v_v[i] = total
         for h in range(2):
@@ -253,36 +249,30 @@
     for e in (2, 1, 3):
         swaps.append(send(sens_v.at[mod4(y + e)], sens_x.at[0, :, :, e * 128 : (e + 1) * 128], along(1, e)))
         swaps.append(send(sens_v.at[:, mod4(x + e)], sens_x.at[1, :, :, e * 128 : (e + 1) * 128], along(0, e)))
+    old = len(sent)
     relay(0)
     collect(0)
     shifts(0)
-    relay(1)
-    collect(1)
-    shifts(1)
-    relay(2)
-    collect(2)
-    second(0)
-    shifts(2)
-    second(1)
-    excess(0)
+    for i in range(1, NC):
+        relay(i)
+        collect(i)
+        shifts(i)
+    for i in range(NC):
+        second(i)
+    drain(sent[:old])
+    old = len(sent) - 6
+    for i in range(NC):
+        excess(i)
     for c in swaps:
         c.wait_recv()
-    second(2)
-    excess(1)
-    cut(0)
-    excess(2)
-    cut_z(0)
-    cut(1)
-    cut_z(1)
-    cut_last(0)
-    cut(2)
-    cut_last(1)
-    cut_z(2)
-    cut_last(2)
+    drain(sent[:old])
+    for i in range(NC):
+        cut(i)
+    for i in range(NC):
+        cut_last(i)
     for i in range(NC):
         finish(i)
-    for c in sent:
-        c.wait_send()
+    drain(sent)
 
 
 def per_device(base_flow, lodf, dual, rating, sens, fetch_rows, ctg_slot):
@@ -294,14 +284,13 @@
         in_specs=[hbm] * 7,
         out_specs=pl.BlockSpec(memory_space=pltpu.VMEM),
         scratch_shapes=[
-            vm((16, 1, 128), jnp.int32), vm((1, KD), jnp.int32), vm((120, Q), F32), vm((128, Q), BF),
+            vm((1, KD), jnp.int32), vm((120, Q), F32), vm((128, Q), BF),
             vm((KD, ML), BF), vm((KD, ML), BF), vm((16, 128), F32), vm((4, 4, 128, 128), BF), vm((2, 4, 128, 512), BF),
             vm((KD, MP), BF), vm((2048, KD), BF),
-            vm((256, 128), BF), vm((256, 128), BF), vm((NC, 256, 128), BF), vm((NC, 8, 256, 128), BF), vm((NC, 128, KD), BF),
+            vm((16, 16, 1, 128), jnp.int32), vm((NC, 256, 128), BF), vm((NC, 8, 256, 128), BF), vm((NC, 128, KD), BF),
             vm((NC, 2, 4, 4, HR, 128), BF), vm((NC, 2, 3, 4, HR, 128), BF), vm((NC, 2, 4, HR, 128), F32),
             vm((NC, 2, 4, HR, 128), BF), vm((NC, 2, 3, HR, 128), BF), vm((NC, 2, HR, 512), BF),
-            vm((NC, 4, 4, 2, 16, 128), F32), vm((NC, 4, 4, 16, 128), F32), vm((NC, 4, 4, 16, 128), F32),
-            vm((NC, 4, 4, 16, 128), BF), vm((NC, 3, 4, 16, 128), BF), vm((NC, 4, 16, 128), F32), vm((NC, 2, 3, 16, 128), F32),
+            vm((NC, 4, 8, 16, 128), F32), vm((NC, 4, 8, 16, 128), BF), vm((NC, 7, 4, 16, 128), BF), vm((NC, 4, 16, 128), F32), vm((NC, 2, 3, 16, 128), F32),
             pltpu.SemaphoreType.DMA((10,)), pltpu.SemaphoreType.DMA((N_SEM,)), pltpu.SemaphoreType.DMA((N_SEM,)),
         ],
         compiler_params=pltpu.CompilerParams(

time: 59.9 us -> 58.4 us (0.975)
  Pallas kernels: 58.4 us -> 56.5 us
    pallas_call x1, Pallas kernels: 58.4 us -> 56.5 us  [per_device(): pl.pallas_call(kernel, out_shape=jax.ShapeDtypeStruct((16, Q), F32), in_s...]
where the time goes in v3:
time: 58.4 us; the launch traced here: 57.8 us
  Pallas kernels  56.5 us (97%)
  local copies, waits for them, and re-layouts  1.35 us (2%)
    pallas_call x1, Pallas kernels, per_device(): pl.pallas_call(kernel, out_shape=jax.ShapeDtypeStruct((16, Q), F32), in_s...  56.5 us
    unnamed x1, local copies, waits for them, and re-layouts  1.35 us

profile of v3, /device:TPU:0, one launch (start us, length us, event | category | flops | bytes accessed | tf_op | source)
XLA Modules:
  0.0 57.8 jit_solution(17325068890235606282)
XLA Ops:
  0.0 56.5 %shard_map.73 = f32[16,384]{1,0:T(8,128)} custom-call(s32[15,1,128]{2,1,0:T(1,128)} %bitcast.12, s32[1,960]{1,0:T(1,128)} %bitcast.13, f32[120,384]{1,0:T(8,128)} %bitcast.10, bf16[960,1920]{1,0:T(8,128)(2,1)} %bitcast.7, bf16[960,1920]{1,0:T(8,128)(2,1)} %bitcast.8, f32[15,128]{1,0:T(8,128)} %bitcast.11, bf16[15,128,128]{2,1,0:T(8,128)(2,1)} %bitcast.9), custom_call_target="tpu_custom_call" | custom-call | tf_op jit(solution)/shard_map/pallas_call | solution.py:281
  56.5 1.3 %copy.9 = f32[16,384]{1,0:T(8,128)} copy(f32[16,384]{1,0:T(8,128)} %shard_map.73) | data formatting | bytes 49152

commit v4 on v3

--- a/solution.py
+++ b/solution.py
@@ -27,8 +27,8 @@
 
 def kernel(
     fr_h, slot_h, base_h, lodf_h, dual_h, rating_h, sens_h, out_ref,
-    slot_v, base_v, base_b, lodf_v, dual_v, rating_v, sens_v, sens_x, w_v, hot,
-    ask_r, val_s, slots, of_b,
+    fr_v, slot_v, base_v, base_b, lodf_v, dual_v, rating_v, sens_v, sens_x, w_v, hot,
+    ask_s, ask_r, val_s, slots, of_b,
     s1, r1, t2, s2, r2, ex, part, zs, zr, v_v, rr,
     load_sem, send_sem, recv_sem,
 ):
@@ -63,13 +63,13 @@
     peers = [mod4(y + a) * 4 + mod4(x + b) for a, b in steps]
 
     loads = {}
-    plan = [("base", base_h, base_v), ("slot", slot_h, slot_v),
+    plan = [("fr", fr_h, fr_v.at[0:15]), ("base", base_h, base_v), ("slot", slot_h, slot_v),
             ("lodf", lodf_h, lodf_v), ("dual", dual_h, dual_v),
             ("sens0", sens_h.at[0:4], sens_v.at[0]), ("sens1", sens_h.at[4:8], sens_v.at[1]),
             ("sens2", sens_h.at[8:12], sens_v.at[2]), ("sens3", sens_h.at[12:15], sens_v.at[3, 0:3]),
             ("rating", rating_h, rating_v.at[0:15])]
     for i, (name, src, dst) in enumerate(plan):
-        loads[name] = pltpu.make_async_copy(src, dst, load_sem.at[i + 1])
+        loads[name] = pltpu.make_async_copy(src, dst, load_sem.at[i])
         loads[name].start()
 
     barrier = pltpu.get_barrier_semaphore()
@@ -79,11 +79,12 @@
         pl.semaphore_signal(barrier, inc=1, device_id=(ctg, lax.rem(line + e, 8)), device_id_type=MESH)
 
     mine = pl.ds(pl.multiple_of(ctg * 16, 16), 16)
+    loads["fr"].wait()
+    fr_v[15] = jnp.full((1, 128), -1, jnp.int32)
+    ask_s[...] = fr_v[...].reshape(16, 128).astype(F32).astype(BF)
+    ask_r[mine, :] = ask_s[...]
     pl.semaphore_wait(barrier, 22)
-    asks = [send(fr_h, ask_r.at[ctg, 0:15], (p, line)) for p in peers]
-    own_ask = pltpu.make_async_copy(fr_h, ask_r.at[ctg, 0:15], load_sem.at[0])
-    own_ask.start()
-    ask_r[:, 15:16] = jnp.full((16, 1, 1, 128), -1, jnp.int32)
+    asks = [send(ask_s, ask_r.at[mine, :], (p, line)) for p in peers]
 
     loads["base"].wait()
     base_b[0:112, :] = base_v[0:112, :].astype(BF)
@@ -106,9 +107,8 @@
 
     for a in asks:
         a.wait_recv()
-    own_ask.wait()
     lane = lax.broadcasted_iota(jnp.int32, (256, 128), 1)
-    wanted = jnp.where(lane == ctg * 8 + line, ask_r[...].reshape(256, 128), 0).astype(BF)
+    wanted = jnp.where(lane == ctg * 8 + line, ask_r[...].astype(F32), 0.0).astype(BF)
     wanted = jnp.dot(wanted, jnp.ones((128, 128), BF), preferred_element_type=F32)
     pick = jnp.where(wanted == lane.astype(F32), 1.0, 0.0).astype(BF)
     found = jnp.dot(pick, base_b[...], preferred_element_type=F32).astype(BF)
@@ -252,11 +252,13 @@
     old = len(sent)
     relay(0)
     collect(0)
+    relay(1)
     shifts(0)
-    for i in range(1, NC):
-        relay(i)
-        collect(i)
-        shifts(i)
+    collect(1)
+    relay(2)
+    shifts(1)
+    collect(2)
+    shifts(2)
     for i in range(NC):
         second(i)
     drain(sent[:old])
@@ -284,10 +286,10 @@
         in_specs=[hbm] * 7,
         out_specs=pl.BlockSpec(memory_space=pltpu.VMEM),
         scratch_shapes=[
-            vm((1, KD), jnp.int32), vm((120, Q), F32), vm((128, Q), BF),
+            vm((16, 1, 128), jnp.int32), vm((1, KD), jnp.int32), vm((120, Q), F32), vm((128, Q), BF),
             vm((KD, ML), BF), vm((KD, ML), BF), vm((16, 128), F32), vm((4, 4, 128, 128), BF), vm((2, 4, 128, 512), BF),
             vm((KD, MP), BF), vm((2048, KD), BF),
-            vm((16, 16, 1, 128), jnp.int32), vm((NC, 256, 128), BF), vm((NC, 8, 256, 128), BF), vm((NC, 128, KD), BF),
+            vm((16, 128), BF), vm((256, 128), BF), vm((NC, 256, 128), BF), vm((NC, 8, 256, 128), BF), vm((NC, 128, KD), BF),
             vm((NC, 2, 4, 4, HR, 128), BF), vm((NC, 2, 3, 4, HR, 128), BF), vm((NC, 2, 4, HR, 128), F32),
             vm((NC, 2, 4, HR, 128), BF), vm((NC, 2, 3, HR, 128), BF), vm((NC, 2, HR, 512), BF),
             vm((NC, 4, 8, 16, 128), F32), vm((NC, 4, 8, 16, 128), BF), vm((NC, 7, 4, 16, 128), BF), vm((NC, 4, 16, 128), F32), vm((NC, 2, 3, 16, 128), F32),

time: 58.4 us -> 57.9 us (level)
  no operation moved by 1% of the time
where the time goes in v4:
time: 57.9 us; the launch traced here: 57.7 us
  Pallas kernels  56.4 us (97%)
  local copies, waits for them, and re-layouts  1.35 us (2%)
    pallas_call x1, Pallas kernels, per_device(): pl.pallas_call(kernel, out_shape=jax.ShapeDtypeStruct((16, Q), F32), in_s...  56.4 us
    unnamed x1, local copies, waits for them, and re-layouts  1.35 us

profile of v4, /device:TPU:0, one launch (start us, length us, event | category | flops | bytes accessed | tf_op | source)
XLA Modules:
  0.0 57.7 jit_solution(16320291553201513393)
XLA Ops:
  0.0 56.4 %shard_map.73 = f32[16,384]{1,0:T(8,128)} custom-call(s32[15,1,128]{2,1,0:T(1,128)} %bitcast.12, s32[1,960]{1,0:T(1,128)} %bitcast.13, f32[120,384]{1,0:T(8,128)} %bitcast.10, bf16[960,1920]{1,0:T(8,128)(2,1)} %bitcast.7, bf16[960,1920]{1,0:T(8,128)(2,1)} %bitcast.8, f32[15,128]{1,0:T(8,128)} %bitcast.11, bf16[15,128,128]{2,1,0:T(8,128)(2,1)} %bitcast.9), custom_call_target="tpu_custom_call" | custom-call | tf_op jit(solution)/shard_map/pallas_call | solution.py:283
  56.4 1.3 %copy.9 = f32[16,384]{1,0:T(8,128)} copy(f32[16,384]{1,0:T(8,128)} %shard_map.73) | data formatting | bytes 49152

commit v5 on v4

--- a/solution.py
+++ b/solution.py
@@ -14,7 +14,7 @@
 KD = 960
 ML = 1920
 MP = 2048
-N_SEM = 160
+N_SEM = 176
 
 
 def mod4(v):
@@ -117,7 +117,11 @@
     vals = []
     for p in peers:
         theirs = pl.ds(pl.multiple_of(p * 16, 16), 16)
-        vals.append(send(val_s.at[:, theirs, :], slots.at[:, 0, mine, :], (p, line)))
+        vals.append(send(val_s.at[0, theirs, :], slots.at[0, 0, mine, :], (p, line)))
+    rest = []
+    for p in peers:
+        theirs = pl.ds(pl.multiple_of(p * 16, 16), 16)
+        rest.append(send(val_s.at[1:3, theirs, :], slots.at[1:3, 0, mine, :], (p, line)))
     for i in range(NC):
         slots[i, 0, mine, :] = val_s[i, mine, :]
 
@@ -243,8 +247,11 @@
             total = total + jnp.where(lane_o < HR, rr[i, 0, e], rr[i, 1, e])
         out_ref[:, i * 128 : (i + 1) * 128] = total
 
-    for i in range(NC):
-        gather(i)
+    gather(0)
+    for v in rest:
+        v.wait_recv()
+    gather(1)
+    gather(2)
     swaps = []
     for e in (2, 1, 3):
         swaps.append(send(sens_v.at[mod4(y + e)], sens_x.at[0, :, :, e * 128 : (e + 1) * 128], along(1, e)))

time: 57.9 us -> 57.9 us (level)
  no operation moved by 1% of the time
where the time goes in v5:
time: 57.9 us; the launch traced here: 57.8 us
  Pallas kernels  56.4 us (97%)
  local copies, waits for them, and re-layouts  1.35 us (2%)
    pallas_call x1, Pallas kernels, per_device(): pl.pallas_call(kernel, out_shape=jax.ShapeDtypeStruct((16, Q), F32), in_s...  56.4 us
    unnamed x1, local copies, waits for them, and re-layouts  1.35 us

profile of v5, /device:TPU:0, one launch (start us, length us, event | category | flops | bytes accessed | tf_op | source)
XLA Modules:
  0.0 57.8 jit_solution(4489807904799131498)
XLA Ops:
  0.0 56.4 %shard_map.73 = f32[16,384]{1,0:T(8,128)} custom-call(s32[15,1,128]{2,1,0:T(1,128)} %bitcast.12, s32[1,960]{1,0:T(1,128)} %bitcast.13, f32[120,384]{1,0:T(8,128)} %bitcast.10, bf16[960,1920]{1,0:T(8,128)(2,1)} %bitcast.7, bf16[960,1920]{1,0:T(8,128)(2,1)} %bitcast.8, f32[15,128]{1,0:T(8,128)} %bitcast.11, bf16[15,128,128]{2,1,0:T(8,128)(2,1)} %bitcast.9), custom_call_target="tpu_custom_call" | custom-call | tf_op jit(solution)/shard_map/pallas_call | solution.py:290
  56.4 1.3 %copy.9 = f32[16,384]{1,0:T(8,128)} copy(f32[16,384]{1,0:T(8,128)} %shard_map.73) | data formatting | bytes 49152
